TPU v7x, 32 devices: a whole 2x2x4 slice. The times are simulated.
32 devices in a mesh: groups: 2 (over y), wide: 4 (over x, core), narrow: 4 (over z).
Axes of the slice: x: 2, y: 2, z: 4, core: 2. Of those that a mesh axis runs over, the one named last changes fastest.
Arguments:
- centers: bfloat16 [8192, 1280], P(('groups', 'wide')), parts along dimension 0, may hold values from -6 to 6
- coefs: float32 [8192, 1000], P(('groups', 'wide', 'narrow')), parts along dimension 0, may hold values from -6 to 6
- slots: int32 [8, 1024], P(('groups', 'wide')), parts along dimension 0, may hold values from 0 to 1023, each once within a row
- pool: bfloat16 [8, 1024, 1280], P(('groups', 'narrow')), parts along dimension 0, may hold values from -6 to 6
- labels: bfloat16 [8, 1024, 1000], P(('groups', 'narrow')), parts along dimension 0, may hold values from -6 to 6
- order: int32 [8, 1024], P(('groups', 'narrow')), parts along dimension 0, may hold values from 0 to 1023, each once within a row
Outputs:
- new_coefs: float32 [8192, 1000], P(('groups', 'wide', 'narrow')), parts along dimension 0
- last_residual: bfloat16 [8, 512, 1000], P(('groups', 'narrow'), 'wide'), parts along dimension 0
There are 2 independent parts, one for each index of `groups`. A program takes and returns all parts, laid end to end along the dimension named above; each array names one. Nothing has to cross between parts.
Inputs may be any that keep to these rules, and one draw needn't show every extreme that they name: Each row of slots is a permutation of the slots of one shard. Each row of order names every sample of its member once.
All inputs are finite; a program needn't handle non-finite values.
Results may differ from a plain program's by a relative error of at most 0.008.
Values may be sent and summed in bfloat16 or wider, within the bound.
A program may use at most 64 MiB of HBM per device.

v0:
```python
import math

import jax
import jax.numpy as jnp
from jax import lax
from jax.sharding import PartitionSpec as P

INNER = 2


def unit_rows(values):
    widened = values.astype(jnp.float32)
    scale = lax.rsqrt(jnp.sum(widened * widened, axis=-1, keepdims=True) + 1e-06)
    return (widened * scale).astype(jnp.bfloat16)


def kernel_block(left, right, sharpness):
    cosine = lax.dot_general(
        left, right, (((1,), (1,)), ((), ())), preferred_element_type=jnp.float32
    )
    distance = jnp.sqrt(2.0 - 2.0 * cosine + 0.01)
    return jnp.exp((math.sqrt(2.01) - distance) * sharpness).astype(jnp.bfloat16)


def center_grad(kernel_rows, resid):
    return lax.dot_general(
        kernel_rows, resid, (((0,), (0,)), ((), ())), preferred_element_type=jnp.float32
    )


def local(centers, coefs, slots, pool, labels, order):
    width = centers.shape[1]
    cen_local = centers.shape[0]
    sharpness = math.sqrt(width) / 1.5
    wide_count = lax.axis_size("wide")
    inv_root = 1.0 / math.sqrt(cen_local * wide_count)
    batch_rows = order.shape[1] // INNER
    share = batch_rows // wide_count
    my_start = lax.axis_index("wide") * share
    center_unit = unit_rows(jnp.take(centers, slots[0], axis=0))
    coef_full = lax.all_gather(coefs.astype(jnp.bfloat16), "narrow", axis=0, tiled=True)
    kernels = []
    resids = []
    previous_x = None
    previous_r = None
    resid_local = None
    for step in range(INNER):
        batch_ids = order[0, step * batch_rows : (step + 1) * batch_rows]
        xunit = unit_rows(jnp.take(pool[0], batch_ids, axis=0))
        target = jnp.take(labels[0], batch_ids, axis=0)
        kernel_rows = kernel_block(xunit, center_unit, sharpness)

        def partial_rows(start, count, kernel_rows=kernel_rows):
            return jnp.dot(kernel_rows, coef_full, preferred_element_type=jnp.float32) * inv_root

        predicted = lax.psum_scatter(
            partial_rows(jnp.int32(0), share * lax.axis_size("wide")),
            "wide",
            scatter_dimension=0,
            tiled=True,
        )
        my_x = lax.dynamic_slice_in_dim(xunit, my_start, share, 0)
        my_target = lax.dynamic_slice_in_dim(target, my_start, share, 0).astype(jnp.float32)
        if step > 0:
            local_kern = kernel_block(my_x, previous_x, sharpness)
            predicted = predicted - 2.0 / batch_rows * jnp.dot(
                local_kern, previous_r, preferred_element_type=jnp.float32
            )
        resid_local = (predicted - my_target).astype(jnp.bfloat16)
        resid_full = lax.all_gather(resid_local, "wide", axis=0, tiled=True)
        kernels.append(kernel_rows)
        resids.append(resid_full)
        previous_x = xunit
        previous_r = resid_full
    summed = center_grad(kernels[0], resids[0])
    summed = summed + center_grad(kernels[1], resids[1])
    owned_grad = lax.psum_scatter(
        summed.astype(jnp.bfloat16), "narrow", scatter_dimension=0, tiled=True
    ).astype(jnp.float32)
    new_coefs = coefs - 0.5 * inv_root * owned_grad
    return (new_coefs, resid_local[None])


def solution(mesh):
    return jax.shard_map(
        local,
        mesh=mesh,
        in_specs=(
            P(("groups", "wide"), None),
            P(("groups", "wide", "narrow"), None),
            P(("groups", "wide"), None),
            P(("groups", "narrow"), None, None),
            P(("groups", "narrow"), None, None),
            P(("groups", "narrow"), None),
        ),
        out_specs=(P(("groups", "wide", "narrow"), None), P(("groups", "narrow"), "wide", None)),
        check_vma=False,
    )
```

profile of v0, /device:TPU:0, one launch (start us, length us, event | category | flops | bytes accessed | tf_op | source)
XLA Modules:
  0.0 196.4 jit_solution(6262011778633139807)
XLA Ops:
  7.2 2.2 %convert_element_type.53 = bf16[256,1000]{0,1:T(8,128)(2,1)} convert(f32[256,1000]{0,1:T(8,128)} %param.11) | non-fusion elementwise | flops 256000 | bytes 1536000 | tf_op jit(solution)/shard_map/convert_element_type | solution.py:41
  10.2 2.9 %gather_fusion.1 = bf16[512,1280]{1,0:T(8,128)(2,1)} fusion(bf16[1024,1280]{1,0:T(8,128)(2,1)S(1)} %bitcast.19, s32[1024]{0:T(1024)S(1)} %pad_clamp_fusion.1), kind=kCustom, calls=%fused_computation.clone | custom fusion | bytes 2623488 | tf_op jit(solution)/shard_map/jit(_take)/gather | solution.py:49
  13.1 8.7 %gather_fusion = bf16[1024,1280]{1,0:T(8,128)(2,1)} fusion(bf16[1024,1280]{1,0:T(8,128)(2,1)} %param.10, s32[1024]{0:T(1024)S(1)} %broadcast_clamp_fusion), kind=kCustom, calls=%fused_computation.4 | custom fusion | bytes 5246976 | tf_op jit(solution)/shard_map/jit(_take)/gather | solution.py:40
  21.9 2.0 %fusion.2 = f32[512]{0:T(512)S(1)} fusion(bf16[512,1280]{1,0:T(8,128)(2,1)} %gather_fusion.1, pred[512]{0:T(512)(128)(4,1)S(1)} %compare_and_fusion.2), kind=kLoop, calls=%fused_computation.14 | loop fusion | flops 2620928 | bytes 1313280 | tf_op jit(solution)/shard_map/reduce_sum | solution.py:13
  23.9 2.6 %fusion = f32[1024]{0:T(1024)S(1)} fusion(bf16[1024,1280]{1,0:T(8,128)(2,1)} %gather_fusion, pred[1024]{0:T(1024)(128)(4,1)S(1)} %compare_and_fusion), kind=kLoop, calls=%fused_computation.7 | loop fusion | flops 5241856 | bytes 2626560 | tf_op jit(solution)/shard_map/reduce_sum | solution.py:13
  26.5 3.5 %exponential_convert_fusion.1 = bf16[512,1024]{1,0:T(8,128)(2,1)} fusion(f32[512]{0:T(512)S(1)} %add_rsqrt_fusion.2, bf16[512,1280]{1,0:T(8,128)(2,1)S(1)} %copy-done.4, pred[512]{0:T(512)(128)(4,1)S(1)} %compare_and_fusion.2, f32[1024]{0:T(1024)S(1)} %add_rsqrt_fusion, bf16[1024,1280]{1,0:T(8,128)(2,1)S(1)} %copy-done.2, ...), kind=kOutput, calls=%fused_computation.20 | convolution fusion | flops 1352663040 | bytes 4988416 | tf_op jit(solution)/shard_map/dot_general | solution.py:18
  30.0 28.3 %all-gather.2.cloned.1.call-done = bf16[1024,1000]{0,1:T(8,128)(2,1)} async-done(((bf16[256,1000]{0,1:T(8,128)(2,1)}), bf16[1024,1000]{0,1:T(8,128)(2,1)}) %all-gather.2.cloned.1.call-update) | async-done | bytes 2048016 | tf_op jit(solution)/shard_map/all_gather | solution.py:41
  58.3 4.5 %convolution_multiply_fusion.1 = f32[512,1000]{0,1:T(8,128)} fusion(bf16[512,1024]{1,0:T(8,128)(2,1)} %exponential_convert_fusion.1, bf16[1024,1000]{0,1:T(8,128)(2,1)} %all-gather.2.cloned.1.call-done), kind=kOutput, calls=%fused_computation.22 | convolution fusion | flops 1049088000 | bytes 5144576 | tf_op jit(solution)/shard_map/dot_general | solution.py:54
  62.9 2.9 %gather_fusion.3 = bf16[512,1280]{1,0:T(8,128)(2,1)} fusion(bf16[1024,1280]{1,0:T(8,128)(2,1)S(1)} %bitcast.20, s32[1024]{0:T(1024)S(1)} %pad_clamp_fusion), kind=kCustom, calls=%fused_computation.2.clone | custom fusion | bytes 2623488 | tf_op jit(solution)/shard_map/jit(_take)/gather | solution.py:49
  65.8 2.1 %fusion.4 = f32[512]{0:T(512)S(1)} fusion(bf16[512,1280]{1,0:T(8,128)(2,1)} %gather_fusion.3, pred[512]{0:T(512)(128)(4,1)S(1)} %compare_and_fusion.1), kind=kLoop, calls=%fused_computation.16 | loop fusion | flops 2620928 | bytes 1313280 | tf_op jit(solution)/shard_map/reduce_sum | solution.py:13
  68.6 3.1 %exponential_convert_fusion = bf16[512,1024]{1,0:T(8,128)(2,1)S(1)} fusion(bf16[512,1280]{1,0:T(8,128)(2,1)S(1)} %fusion.5, f32[1024]{0:T(1024)S(1)} %add_rsqrt_fusion, bf16[1024,1280]{1,0:T(8,128)(2,1)S(1)} %copy-done.3, pred[1024]{0:T(1024)(128)(4,1)S(1)} %compare_and_fusion), kind=kOutput, calls=%fused_computation.19 | convolution fusion | flops 1350041600 | bytes 4985856 | tf_op jit(solution)/shard_map/dot_general | solution.py:18
  72.7 2.6 %convolution_multiply_fusion = f32[512,1000]{0,1:T(8,128)} fusion(bf16[512,1024]{1,0:T(8,128)(2,1)S(1)} %exponential_convert_fusion, bf16[1024,1000]{0,1:T(8,128)(2,1)S(1)} %copy-done.11), kind=kOutput, calls=%fused_computation.21 | convolution fusion | flops 1049088000 | bytes 5144576 | tf_op jit(solution)/shard_map/dot_general | solution.py:54
  75.8 3.9 %copy.11 = bf16[1,1024,1000]{2,1,0:T(8,128)(2,1)} copy(bf16[1,1024,1000]{1,2,0:T(8,128)(2,1)} %param.14) | data formatting | bytes 4096000 | tf_op args[4]
  79.7 5.3 %gather_fusion.4 = bf16[512,1000]{1,0:T(8,128)(2,1)} fusion(bf16[1024,1000]{1,0:T(8,128)(2,1)} %bitcast.21, s32[1024]{0:T(1024)S(1)} %pad_clamp_fusion), kind=kCustom, calls=%fused_computation.3.clone | custom fusion | bytes 2050048 | tf_op jit(solution)/shard_map/jit(_take)/gather | solution.py:50
  85.0 5.4 %gather_fusion.2 = bf16[512,1000]{1,0:T(8,128)(2,1)} fusion(bf16[1024,1000]{1,0:T(8,128)(2,1)} %bitcast.22, s32[1024]{0:T(1024)S(1)} %pad_clamp_fusion.1), kind=kCustom, calls=%fused_computation.1.clone | custom fusion | bytes 2050048 | tf_op jit(solution)/shard_map/jit(_take)/gather | solution.py:50
  92.8 1.2 subtract_convert_fusion
  94.0 10.0 %all_gather.10 = bf16[512,1000]{0,1:T(8,128)(2,1)S(1)} all-gather(bf16[128,1000]{0,1:T(8,128)(2,1)S(1)} %subtract_convert_fusion), channel_id=1, replica_groups=mesh['groups'=2,'wide'=4,'narrow'=4] {'wide'}, dimensions={0}, use_global_device_ids=true | all-gather | bytes 1280000 | tf_op jit(solution)/shard_map/all_gather | solution.py:70
  105.0 3.3 %fusion.33 = f32[1024,1000]{0,1:T(8,128)} fusion(bf16[512,1024]{1,0:T(8,128)(2,1)S(1)} %copy-done.6, bf16[512,1000]{0,1:T(8,128)(2,1)S(1)} %all_gather.10), kind=kOutput, calls=%fused_computation.64 | convolution fusion | flops 1048576000 | bytes 6168576 | tf_op jit(solution)/shard_map/dot_general | solution.py:26
  108.3 18.0 %reduce-scatter.6.cloned.1.call-done = f32[128,1000]{0,1:T(8,128)} async-done(((f32[512,1000]{0,1:T(8,128)}), f32[128,1000]{0,1:T(8,128)}) %reduce-scatter.6.cloned.1.call-update) | async-done | bytes 512016 | tf_op jit(solution)/shard_map/reduce_scatter | solution.py:56
  126.3 3.1 %fusion.8 = bf16[128,1000]{0,1:T(8,128)(2,1)S(1)} fusion(f32[128,1000]{0,1:T(8,128)} %reduce-scatter.6.cloned.1.call-done, bf16[512,1000]{0,1:T(8,128)(2,1)} %copy-done.5, bf16[512,1280]{1,0:T(8,128)(2,1)} %copy-done.7, s32[]{:T(128)S(6)} %select_n.41, bf16[128,1000]{0,1:T(8,128)(2,1)S(1)} %copy.15, pred[128]{0:T(512)(128)(4,1)S(1)} %dynamic-slice.1, ...), kind=kOutput, calls=%fused_computation.28 | convolution fusion | flops 302561280 | bytes 3689092 | tf_op jit(solution)/shard_map/dot_general | solution.py:66
  129.3 9.5 %all_gather.11 = bf16[512,1000]{0,1:T(8,128)(2,1)S(1)} all-gather(bf16[128,1000]{0,1:T(8,128)(2,1)S(1)} %fusion.8), channel_id=1, replica_groups=mesh['groups'=2,'wide'=4,'narrow'=4] {'wide'}, dimensions={0}, use_global_device_ids=true | all-gather | bytes 1280000 | tf_op jit(solution)/shard_map/all_gather | solution.py:70
  138.9 5.0 %add_convert_fusion = bf16[1024,1000]{0,1:T(8,128)(2,1)} fusion(f32[1024,1000]{0,1:T(8,128)} %fusion.33, bf16[512,1024]{1,0:T(8,128)(2,1)} %copy-done.8, bf16[512,1000]{0,1:T(8,128)(2,1)S(1)} %all_gather.11), kind=kOutput, calls=%fused_computation.9 | convolution fusion | flops 1050624000 | bytes 8216576 | tf_op jit(solution)/shard_map/dot_general | solution.py:26
  143.9 43.6 %reduce-scatter.8.cloned.1.call-done = bf16[256,1000]{0,1:T(8,128)(2,1)} async-done(((bf16[1024,1000]{0,1:T(8,128)(2,1)}), bf16[256,1000]{0,1:T(8,128)(2,1)}) %reduce-scatter.8.cloned.1.call-update) | async-done | bytes 512016 | tf_op jit(solution)/shard_map/reduce_scatter | solution.py:77
  187.5 2.4 %multiply_subtract_fusion = f32[256,1000]{0,1:T(8,128)} fusion(f32[256,1000]{0,1:T(8,128)} %param.11, bf16[256,1000]{0,1:T(8,128)(2,1)} %reduce-scatter.8.cloned.1.call-done), kind=kLoop, calls=%fused_computation.36 | loop fusion | flops 768000 | bytes 2560000 | tf_op jit(solution)/shard_map/sub | solution.py:80
  (53 shorter events, 6.4 us)
Async XLA Ops:
  7.2 3.1 %copy-start = (bf16[1,1024,1280]{2,1,0:T(8,128)(2,1)S(1)}, bf16[1,1024,1280]{2,1,0:T(8,128)(2,1)}, u32[]{:S(2)}) copy-start(bf16[1,1024,1280]{2,1,0:T(8,128)(2,1)} %param.13) | copy-start | bytes 7864324
  7.2 51.1 %all-gather.2.cloned.1.call-start = ((), (), s32[]{:S(2)}) async-start(), calls=%async_computation.3 | async-start | bytes 2560000 | tf_op jit(solution)/shard_map/all_gather | solution.py:41
  9.5 83.3 %reduce-scatter.4.cloned.1.call-start = ((), (), s32[]{:S(2)}) async-start(), calls=%async_computation.4 | async-start | bytes 2560000 | tf_op jit(solution)/shard_map/reduce_scatter | solution.py:56
  10.2 2.9 %copy-start.10 = (s32[1,1024]{1,0:T(1,128)S(1)}, s32[1,1024]{1,0:T(1,128)}, u32[]{:S(2)}) copy-start(s32[1,1024]{1,0:T(1,128)} %param.12) | copy-start | bytes 12292
  21.8 4.6 %copy-start.2 = (bf16[1024,1280]{1,0:T(8,128)(2,1)S(1)}, bf16[1024,1280]{1,0:T(8,128)(2,1)}, u32[]{:S(2)}) copy-start(bf16[1024,1280]{1,0:T(8,128)(2,1)} %gather_fusion) | copy-start | bytes 7864324
  21.8 4.6 %copy-start.4 = (bf16[512,1280]{1,0:T(8,128)(2,1)S(1)}, bf16[512,1280]{1,0:T(8,128)(2,1)}, u32[]{:S(2)}) copy-start(bf16[512,1280]{1,0:T(8,128)(2,1)} %gather_fusion.1) | copy-start | bytes 3932164
  62.9 63.4 %reduce-scatter.6.cloned.1.call-start = ((), (), s32[]{:S(2)}) async-start(), calls=%async_computation.5 | async-start | bytes 2560000 | tf_op jit(solution)/shard_map/reduce_scatter | solution.py:56
  65.8 2.1 %copy-start.1 = (bf16[512,1280]{1,0:T(8,128)(2,1)S(1)}, bf16[512,1280]{1,0:T(8,128)(2,1)}, u32[]{:S(2)}) copy-start(bf16[512,1280]{1,0:T(8,128)(2,1)} %gather_fusion.3) | copy-start | bytes 3932164
  65.8 2.8 %copy-start.3 = (bf16[1024,1280]{1,0:T(8,128)(2,1)S(1)}, bf16[1024,1280]{1,0:T(8,128)(2,1)}, u32[]{:S(2)}) copy-start(bf16[1024,1280]{1,0:T(8,128)(2,1)} %gather_fusion) | copy-start | bytes 7864324
  68.6 3.1 %copy-start.7 = (bf16[512,1280]{1,0:T(8,128)(2,1)}, bf16[512,1280]{1,0:T(8,128)(2,1)S(1)}, u32[]{:S(2)}) copy-start(bf16[512,1280]{1,0:T(8,128)(2,1)S(1)} %fusion.5) | copy-start | bytes 3932164
  68.6 4.1 %copy-start.11 = (bf16[1024,1000]{0,1:T(8,128)(2,1)S(1)}, bf16[1024,1000]{0,1:T(8,128)(2,1)}, u32[]{:S(2)}) copy-start(bf16[1024,1000]{0,1:T(8,128)(2,1)} %all-gather.2.cloned.1.call-done) | copy-start | bytes 6144004
  71.7 1.0 copy-start.8
  75.4 112.1 %reduce-scatter.8.cloned.1.call-start = ((), (), s32[]{:S(2)}) async-start(), calls=%async_computation.6 | async-start | bytes 2560000 | tf_op jit(solution)/shard_map/reduce_scatter | solution.py:77
  92.8 12.2 %copy-start.6 = (bf16[512,1024]{1,0:T(8,128)(2,1)S(1)}, bf16[512,1024]{1,0:T(8,128)(2,1)}, u32[]{:S(2)}) copy-start(bf16[512,1024]{1,0:T(8,128)(2,1)} %exponential_convert_fusion.1) | copy-start | bytes 3145732
  104.0 1.0 copy-start.5
  129.3 14.6 %copy-start.9 = (bf16[128,1000]{0,1:T(8,128)(2,1)}, bf16[128,1000]{0,1:T(8,128)(2,1)S(1)}, u32[]{:S(2)}) copy-start(bf16[128,1000]{0,1:T(8,128)(2,1)S(1)} %fusion.8) | copy-start | bytes 768004
Sparse Core Ops, SparseCore 0:
  10.1 48.1 all-gather.1
  63.0 29.3 reduce-scatter.3
  95.1 31.1 reduce-scatter.5
  144.1 43.4 reduce-scatter.7
where the time goes:
time: 197 us; the launch traced here: 196 us
  waiting for transfers between devices  90 us (46%)
  local copies, waits for them, and re-layouts  34.5 us (18%)
  matrix products  25.2 us (13%)
  blocking collectives  19.5 us (10%)
  between operations  13.9 us (7%)
  other arithmetic  12.9 us (7%)
    reduce_scatter x1, waiting for transfers between devices, local(): lax.psum_scatter(summed.astype(jnp.bfloat16), 'narrow', scatter_dimension...  43.6 us
    all_gather x1, waiting for transfers between devices, local(): lax.all_gather(coefs.astype(jnp.bfloat16), 'narrow', axis=0, tiled=True)  28.3 us
    all_gather x2, blocking collectives, local(): resid_full = lax.all_gather(resid_local, 'wide', axis=0, tiled=True)  19.5 us
    reduce_scatter x2, waiting for transfers between devices, local(): lax.psum_scatter(partial_rows(jnp.int32(0), share * lax.axis_size('wide')...  18 us
    gather x2, local copies, waits for them, and re-layouts, local(): target = jnp.take(labels[0], batch_ids, axis=0)  10.7 us
    gather x1, local copies, waits for them, and re-layouts, local(): center_unit = unit_rows(jnp.take(centers, slots[0], axis=0))  8.7 us
    dot_general x2, matrix products, center_grad(): lax.dot_general(kernel_rows, resid, (((0,), (0,)), ((), ())), preferred_e...  8.34 us
    dot_general x2, matrix products, partial_rows(): jnp.dot(kernel_rows, coef_full, preferred_element_type=jnp.float32)  7.17 us
  transfers between devices with their start and end apart: 4, of which 3 were waited for; matrix products, arithmetic and copies ran while one was open for 27% of the time, Pallas kernels for 0%

commit v1 on v0

v1 whole, which is shorter than its diff:
```python
import functools
import math

import jax
import jax.numpy as jnp
from jax import lax
from jax.experimental import pallas as pl
from jax.experimental.pallas import tpu as pltpu
from jax.sharding import PartitionSpec as P

INNER = 2
WIDTH = 256
F32 = jnp.float32
BF16 = jnp.bfloat16
MESH = pl.DeviceIdType.MESH


def one_hot(column, count):
    lane = lax.broadcasted_iota(jnp.int32, column.shape, 1)
    pieces = [
        jnp.where(column == lane + 128 * g, 1.0, 0.0).astype(BF16) for g in range(count // 128)
    ]
    return jnp.concatenate(pieces, axis=1)


def unit_rows(widened):
    scale = lax.rsqrt(jnp.sum(widened * widened, axis=-1, keepdims=True) + 1e-06)
    return (widened * scale).astype(BF16)


def kernel_block(left, right, sharpness):
    cosine = lax.dot_general(left, right, (((1,), (1,)), ((), ())), preferred_element_type=F32)
    distance = jnp.sqrt(2.0 - 2.0 * cosine + 0.01)
    return jnp.exp((math.sqrt(2.01) - distance) * sharpness).astype(BF16)


def column_of(row):
    return jnp.broadcast_to(row, (128, row.shape[1])).T


def body(
    nw, nz, nc, cen_h, coef_h, slots_h, pool_h, lab_h, order_h, new_ref, last_ref,
    cen, coef, slots, pool, lab, order, slotc, ordc, xu, cu, kx, kt, lk, tgt,
    cbuf, part, prec, xs, xr, rbuf, grad, gs, gr,
    lsem, ag_s, ag_r, pp_s, pp_r, xx_s, xx_r, rr_s, rr_r, rs_s, rs_r,
):
    nx = nw // 2
    batch, centers_n, width = kx.shape[0] // INNER, kx.shape[1], cen.shape[1]
    pool_n, outs = lab.shape[1], coef.shape[1]
    rows, share = coef.shape[0], batch // nw
    half = batch // 2
    sharpness = math.sqrt(width) / 1.5
    inv_root = 1.0 / math.sqrt(centers_n * nw)
    z = lax.axis_index("narrow")
    w = lax.axis_index("wide")
    c, x = lax.rem(w, 2), lax.div(w, 2)
    mate = w + 1 - 2 * c
    spans = [min(WIDTH, outs - j * WIDTH) for j in range(nc)]

    loads = [
        pltpu.make_async_copy(src, dst, lsem.at[i])
        for i, (src, dst) in enumerate(
            [(coef_h, coef), (order_h, order), (pool_h, pool), (slots_h, slots), (cen_h, cen), (lab_h, lab)]
        )
    ]
    for load in loads:
        load.start()

    barrier = pltpu.get_barrier_semaphore()

    def greet(device):
        pl.semaphore_signal(barrier, inc=1, device_id=device, device_id_type=MESH)

    for e in range(1, nw):
        greet({"wide": lax.rem(w + e, nw)})
    pl.when(z > 0)(lambda: greet({"narrow": z - 1}))
    pl.when(z < nz - 1)(lambda: greet({"narrow": z + 1}))

    loads[0].wait()
    for j in range(nc):
        value = coef[:, j * WIDTH : j * WIDTH + spans[j]].astype(BF16)
        if spans[j] < WIDTH:
            cbuf[j, z] = jnp.zeros((rows, WIDTH), BF16)
        cbuf[j, z, :, : spans[j]] = value

    inner = jnp.logical_and(z > 0, z < nz - 1)
    pl.when(inner)(lambda: pl.semaphore_wait(barrier, nw + 1))
    pl.when(jnp.logical_not(inner))(lambda: pl.semaphore_wait(barrier, nw))

    def remote(src, dst, send, recv, device):
        return pltpu.make_async_remote_copy(
            src_ref=src, dst_ref=dst, send_sem=send, recv_sem=recv, device_id=device, device_id_type=MESH
        )

    drains = []

    def gather_copy(j, side, t, shard, to):
        return remote(
            cbuf.at[j, shard], cbuf.at[j, shard], ag_s.at[j, side, t], ag_r.at[j, side, t], {"narrow": to}
        )

    def gather_arrive(j, t):
        @pl.when(z - 1 - t >= 0)
        def _():
            gather_copy(j, 0, t, z - 1 - t, z - 1).wait_recv()

        @pl.when(z + 1 + t <= nz - 1)
        def _():
            gather_copy(j, 1, t, z + 1 + t, z + 1).wait_recv()

    def gather(j, t):
        if t > 0:
            gather_arrive(j, t - 1)
        up = jnp.logical_and(z - t >= 0, z < nz - 1)
        down = jnp.logical_and(z + t <= nz - 1, z > 0)
        pl.when(up)(lambda: gather_copy(j, 0, t, z - t, z + 1).start())
        pl.when(down)(lambda: gather_copy(j, 1, t, z + t, z - 1).start())
        drains.append((up, lambda: gather_copy(j, 0, t, z - t, z + 1).wait_send()))
        drains.append((down, lambda: gather_copy(j, 1, t, z + t, z - 1).wait_send()))

    def indices():
        loads[1].wait()
        column = column_of(order[...])
        for b in range(INNER):
            for v in range(nw):
                at = (b * nw + v) * share
                ordc[2 * b + v % 2, v // 2] = column[at : at + share]

    def sample_rows(i):
        picked = one_hot(ordc[i].reshape(half, 128), pool_n)
        found = jnp.dot(picked, pool[0], preferred_element_type=F32)
        xu[i] = unit_rows(found).reshape(nx, share, width)

    def center_rows(i):
        picked = one_hot(slotc[pl.ds(pl.multiple_of(i * 256, 256), 256)], centers_n)
        found = jnp.dot(picked, cen[...], preferred_element_type=F32)
        cu[pl.ds(pl.multiple_of(i * 256, 256), 256)] = unit_rows(found)

    def kernel_rows(i):
        block = kernel_block(xu[i].reshape(half, width), cu[...], sharpness)
        kx[pl.ds(pl.multiple_of(i * half, half), half)] = block

    def over(count, step):
        lax.fori_loop(0, count, lambda i, carry: (step(i), carry)[1], 0)

    def samples():
        indices()
        loads[2].wait()
        over(2 * INNER, sample_rows)

    def centers():
        loads[3].wait()
        slotc[...] = column_of(slots[...])
        loads[4].wait()
        over(centers_n // 256, center_rows)

    def kernels():
        over(2 * INNER, kernel_rows)

    def turned():
        kt[...] = kx[...].T

    def targets():
        loads[5].wait()
        lk[...] = kernel_block(xu[2 + c, x], xu[0:2].reshape(batch, width), sharpness)
        mine = jnp.concatenate([ordc[c, x], ordc[2 + c, x]], axis=0)
        picked = one_hot(mine, pool_n)
        for j in range(nc):
            if spans[j] < WIDTH:
                tgt[j] = jnp.zeros((INNER * share, WIDTH), F32)
            tgt[j, :, : spans[j]] = jnp.dot(
                picked, lab[0, :, j * WIDTH : j * WIDTH + spans[j]], preferred_element_type=F32
            )

    def mate_copy(j):
        return remote(part.at[j, :, 1 - c], prec.at[j], pp_s.at[j], pp_r.at[j], {"wide": mate})

    def predict(j):
        gather_arrive(j, nz - 2)
        for b in range(INNER):
            product = jnp.dot(
                kx[b * batch : (b + 1) * batch],
                cbuf[j].reshape(centers_n, WIDTH),
                preferred_element_type=F32,
            )
            part[j, b] = (product * inv_root).astype(BF16).reshape(2, nx, share, WIDTH)
        mate_copy(j).start()
        drains.append((None, lambda: mate_copy(j).wait_send()))

    def row_copy(j, d):
        to = lax.rem(x + d, nx)
        return remote(
            xs.at[j, d - 1], xr.at[j, d - 1], xx_s.at[j, d - 1], xx_r.at[j, d - 1], {"wide": 2 * to + c}
        )

    def exchange(j):
        mate_copy(j).wait_recv()
        for d in range(1, nx):
            to = lax.rem(x + d, nx)
            xs[j, d - 1] = (part[j, :, c, to].astype(F32) + prec[j, :, to].astype(F32)).astype(BF16)
            row_copy(j, d).start()
            drains.append((None, lambda d=d: row_copy(j, d).wait_send()))

    def resid_copy(j, b, e):
        block = rbuf.at[j, b, c, x]
        return remote(
            block, block, rr_s.at[j, b, e - 1], rr_r.at[j, b, e - 1], {"wide": lax.rem(w + e, nw)}
        )

    def spread(j, b):
        for e in range(1, nw):
            resid_copy(j, b, e).start()
            drains.append((None, lambda e=e: resid_copy(j, b, e).wait_send()))

    def resid_arrive(j, b):
        for e in range(1, nw):
            source = lax.rem(w + nw - e, nw)
            block = rbuf.at[j, b, lax.rem(source, 2), lax.div(source, 2)]
            remote(
                block, block, rr_s.at[j, b, e - 1], rr_r.at[j, b, e - 1], {"wide": source}
            ).wait_recv()

    def first(j):
        for d in range(1, nx):
            row_copy(j, d).wait_recv()
        total = part[j, :, c, x].astype(F32) + prec[j, :, x].astype(F32)
        for d in range(1, nx):
            total = total + xr[j, d - 1].astype(F32)
        total = total.reshape(INNER * share, WIDTH) - tgt[j]
        rbuf[j, 0, c, x] = total[:share].astype(BF16)
        spread(j, 0)
        tgt[j, share:] = total[share:]

    def second(j):
        resid_arrive(j, 0)
        bent = jnp.dot(lk[...], rbuf[j, 0].reshape(batch, WIDTH), preferred_element_type=F32)
        value = (tgt[j, share:] - 2.0 / batch * bent).astype(BF16)
        rbuf[j, 1, c, x] = value
        spread(j, 1)
        last_ref[0, :, j * WIDTH : j * WIDTH + spans[j]] = value[:, : spans[j]]

    def gradient(j):
        resid_arrive(j, 1)
        size = centers_n // 2
        for h in range(2):
            product = jnp.dot(
                kt[h * size : (h + 1) * size],
                rbuf[j].reshape(INNER * batch, WIDTH),
                preferred_element_type=F32,
            )
            grad[j, h * (nz // 2) : (h + 1) * (nz // 2)] = product.reshape(nz // 2, rows, WIDTH)

    def sum_copy(j, side, t):
        return remote(
            gs.at[j, side, t], gr.at[j, side, t], rs_s.at[j, side, t], rs_r.at[j, side, t],
            {"narrow": z + 1 - 2 * side},
        )

    def reduce_to(j, t):
        for side in range(2):
            rank = z if side == 0 else nz - 1 - z
            slot = nz - 1 - t + z if side == 0 else t - (nz - 1 - z)

            @pl.when(rank == 0)
            def _():
                gs[j, side, t] = grad[j, nz - 1 - t if side == 0 else t].astype(BF16)
                sum_copy(j, side, t).start()

            if t > 0:
                @pl.when(jnp.logical_and(rank >= 1, rank <= t))
                def _():
                    sum_copy(j, side, t - 1).wait_recv()
                    gs[j, side, t] = (grad[j, slot] + gr[j, side, t - 1].astype(F32)).astype(BF16)
                    sum_copy(j, side, t).start()

            drains.append((rank <= t, lambda side=side: sum_copy(j, side, t).wait_send()))

    def finish(j):
        for side in range(2):
            rank = z if side == 0 else nz - 1 - z

            @pl.when(rank >= 1)
            def _():
                sum_copy(j, side, nz - 2).wait_recv()
                grad[j, z] = grad[j, z] + gr[j, side, nz - 2].astype(F32)

        here = slice(j * WIDTH, j * WIDTH + spans[j])
        new_ref[:, here] = coef[:, here] - 0.5 * inv_root * grad[j, z][:, : spans[j]]

    unit = 2 * rows * WIDTH * 2 / 1e5
    steps = []
    for j in range(nc):
        begin = (nz - 1) * unit * j
        for t in range(nz - 1):
            steps.append((begin + t * (unit + 1.0), functools.partial(gather, j, t)))
        now = max(begin + (nz - 1) * (unit + 1.0), 12.0)
        for wait, step in (
            (0.0, predict), (2.0, exchange), (unit + 1.5, first), (unit + 1.5, second), (unit + 1.5, gradient),
        ):
            now += wait
            steps.append((now, functools.partial(step, j)))
        now += 0.5
        for t in range(nz - 1):
            steps.append((now, functools.partial(reduce_to, j, t)))
            now += unit + 1.5
        steps.append((now, functools.partial(finish, j)))
    for at, step in ((0.5, samples), (3.5, centers), (7.0, kernels), (10.5, targets), (11.9, turned)):
        steps.append((at, step))
    for _, step in sorted(steps, key=lambda entry: entry[0]):
        step()
    for condition, drain in drains:
        if condition is None:
            drain()
        else:
            pl.when(condition)(drain)


def local(centers, coefs, slots, pool, labels, order):
    nw, nz = lax.axis_size("wide"), lax.axis_size("narrow")
    nx = nw // 2
    cen_local, width = centers.shape
    rows, outs = coefs.shape
    nc = -(-outs // WIDTH)
    total = order.shape[1]
    batch = total // INNER
    share = batch // nw
    vmem = pltpu.VMEM
    dma = pltpu.SemaphoreType.DMA
    scratch = [
        vmem(centers.shape, BF16),
        vmem(coefs.shape, F32),
        vmem(slots.shape, jnp.int32),
        vmem(pool.shape, BF16),
        vmem(labels.shape, BF16),
        vmem(order.shape, jnp.int32),
        vmem((cen_local, 128), jnp.int32),
        vmem((2 * INNER, nx, share, 128), jnp.int32),
        vmem((2 * INNER, nx, share, width), BF16),
        vmem((cen_local, width), BF16),
        vmem((total, cen_local), BF16),
        vmem((cen_local, total), BF16),
        vmem((share, batch), BF16),
        vmem((nc, INNER * share, WIDTH), F32),
        vmem((nc, nz, rows, WIDTH), BF16),
        vmem((nc, INNER, 2, nx, share, WIDTH), BF16),
        vmem((nc, INNER, nx, share, WIDTH), BF16),
        vmem((nc, nx - 1, INNER, share, WIDTH), BF16),
        vmem((nc, nx - 1, INNER, share, WIDTH), BF16),
        vmem((nc, INNER, 2, nx, share, WIDTH), BF16),
        vmem((nc, nz, rows, WIDTH), F32),
        vmem((nc, 2, nz - 1, rows, WIDTH), BF16),
        vmem((nc, 2, nz - 1, rows, WIDTH), BF16),
        dma((6,)),
        dma((nc, 2, nz - 1)), dma((nc, 2, nz - 1)),
        dma((nc,)), dma((nc,)),
        dma((nc, nx - 1)), dma((nc, nx - 1)),
        dma((nc, INNER, nw - 1)), dma((nc, INNER, nw - 1)),
        dma((nc, 2, nz - 1)), dma((nc, 2, nz - 1)),
    ]
    anywhere = pl.BlockSpec(memory_space=pl.ANY)
    inside = pl.BlockSpec(memory_space=vmem)
    flops = 2 * total * cen_local * (width + 2 * outs)
    return pl.pallas_call(
        functools.partial(body, nw, nz, nc),
        out_shape=(
            jax.ShapeDtypeStruct((rows, outs), F32),
            jax.ShapeDtypeStruct((1, share, outs), BF16),
        ),
        in_specs=[anywhere] * 6,
        out_specs=(inside, inside),
        scratch_shapes=scratch,
        cost_estimate=pl.CostEstimate(
            flops=flops, bytes_accessed=10_000_000, transcendentals=total * cen_local
        ),
        compiler_params=pltpu.CompilerParams(
            collective_id=0, has_side_effects=True, vmem_limit_bytes=52 * 1024 * 1024
        ),
    )(centers, coefs, slots, pool, labels, order)


def solution(mesh):
    return jax.shard_map(
        local,
        mesh=mesh,
        in_specs=(
            P(("groups", "wide"), None),
            P(("groups", "wide", "narrow"), None),
            P(("groups", "wide"), None),
            P(("groups", "narrow"), None, None),
            P(("groups", "narrow"), None, None),
            P(("groups", "narrow"), None),
        ),
        out_specs=(P(("groups", "wide", "narrow"), None), P(("groups", "narrow"), "wide", None)),
        check_vma=False,
    )
```

time: 197 us -> 98 us (0.50)
  waiting for transfers between devices: 90 us -> 0 us
  Pallas kernels: 0 us -> 89.8 us
  local copies, waits for them, and re-layouts: 34.5 us -> 7.39 us
  matrix products: 25.2 us -> 0 us
  blocking collectives: 19.5 us -> 0 us
  between operations: 13.9 us -> 0.67 us
  other arithmetic: 12.9 us -> 0 us
    pallas_call x0 -> x1, Pallas kernels: none -> 89.8 us  [local(): pl.pallas_call(functools.partial(body, nw, nz, nc), out_shape=(jax.ShapeD...]
    reduce_scatter x3 -> x0, waiting for transfers between devices: 61.6 us -> none  [the longest x1 43.6 us: local(): lax.psum_scatter(summed.astype(jnp.bfloat16), 'narrow', scatter_dimension...]
    all_gather x1 -> x0, waiting for transfers between devices: 28.3 us -> none  [local(): lax.all_gather(coefs.astype(jnp.bfloat16), 'narrow', axis=0, tiled=True)]
    dot_general x7 -> x0, matrix products: 25.2 us -> none  [the longest x2 8.34 us: center_grad(): lax.dot_general(kernel_rows, resid, (((0,), (0,)), ((), ())), preferred_e...]
    gather x5 -> x0, local copies, waits for them, and re-layouts: 25.1 us -> none  [the longest x2 10.7 us: local(): target = jnp.take(labels[0], batch_ids, axis=0)]
    all_gather x2 -> x0, blocking collectives: 19.5 us -> none  [local(): resid_full = lax.all_gather(resid_local, 'wide', axis=0, tiled=True)]
    reduce_sum x3 -> x0, other arithmetic: 6.68 us -> none  [unit_rows(): jnp.sum(widened * widened, axis=-1, keepdims=True) + 1e-06]
    convert_element_type x3 -> x0, other arithmetic: 3.78 us -> none  [the longest x1 2.2 us: local(): coefs.astype(jnp.bfloat16)]
  transfers between devices with their start and end apart: 4 -> 0, of which waited for: 3 -> 0; matrix products, arithmetic and copies ran while one was open for 27% -> 0% of each run, Pallas kernels for 0% -> 0%
where the time goes in v1:
time: 98 us; the launch traced here: 97.9 us
  Pallas kernels  89.8 us (92%)
  local copies, waits for them, and re-layouts  7.39 us (8%)
    pallas_call x1, Pallas kernels, local(): pl.pallas_call(functools.partial(body, nw, nz, nc), out_shape=(jax.ShapeD...  89.8 us
    unnamed x8, local copies, waits for them, and re-layouts  5.24 us
    pallas_call x2, local copies, waits for them, and re-layouts, local(): pl.pallas_call(functools.partial(body, nw, nz, nc), out_shape=(jax.ShapeD...  2.15 us

profile of v1, /device:TPU:0, one launch (start us, length us, event | category | flops | bytes accessed | tf_op | source)
XLA Modules:
  0.0 97.9 jit_solution(2634914874985621566)
XLA Ops:
  0.6 0.0 copy-start.1
  0.6 0.0 copy-start.2
  0.7 0.0 copy-start
  0.7 2.7 %copy.8.coef_h = f32[256,1000]{1,0:T(8,128)} copy(f32[256,1000]{0,1:T(8,128)} %param.7) | data formatting | bytes 2048000 | tf_op args[1]
  3.4 0.0 copy-done.2
  3.4 2.5 %copy.9.lab_h = bf16[1,1024,1000]{2,1,0:T(8,128)(2,1)} copy(bf16[1,1024,1000]{1,2,0:T(8,128)(2,1)S(1)} %copy-done.2) | data formatting | bytes 4096000 | tf_op args[4]
  5.9 0.0 copy-done.1
  5.9 0.0 copy-done
  5.9 89.8 %shard_map.77 = (f32[256,1000]{1,0:T(8,128)S(1)}, bf16[1,128,1000]{2,1,0:T(8,128)(2,1)S(1)}) custom-call(bf16[1024,1280]{1,0:T(8,128)(2,1)} %cen_h.1, f32[256,1000]{1,0:T(8,128)} %copy.8.coef_h, s32[1,1024]{1,0:T(1,128)S(1)} %copy-done, bf16[1,1024,1280]{2,1,0:T(8,128)(2,1)} %pool_h.1, bf16[1,1024,1000]{2,1,0:T(8,128)(2,1)} %copy.9.lab_h, ...), custom_call_target="tpu_custom_call" | custom-call | flops 6878658560 | bytes 10000000 | tf_op jit(solution)/shard_map/pallas_call | solution.py:363
  95.7 1.3 %copy.10 = f32[256,1000]{0,1:T(8,128)} copy(f32[256,1000]{1,0:T(8,128)S(1)} %get-tuple-element.2) | data formatting | bytes 2048000 | tf_op jit(solution)/shard_map/pallas_call | solution.py:363
  97.0 0.9 copy.11
Async XLA Ops:
  0.6 5.3 %copy-start.1 = (s32[1,1024]{1,0:T(1,128)S(1)}, s32[1,1024]{1,0:T(1,128)}, u32[]{:S(2)}) copy-start(s32[1,1024]{1,0:T(1,128)} %order_h.1) | copy-start | bytes 12292
  0.6 2.7 %copy-start.2 = (bf16[1,1024,1000]{1,2,0:T(8,128)(2,1)S(1)}, bf16[1,1024,1000]{1,2,0:T(8,128)(2,1)}, u32[]{:S(2)}) copy-start(bf16[1,1024,1000]{1,2,0:T(8,128)(2,1)} %param.10) | copy-start | bytes 6144004
  0.7 5.2 %copy-start = (s32[1,1024]{1,0:T(1,128)S(1)}, s32[1,1024]{1,0:T(1,128)}, u32[]{:S(2)}) copy-start(s32[1,1024]{1,0:T(1,128)} %slots_h.1) | copy-start | bytes 12292
